TPU v7x, 32 devices: a whole 2x2x4 slice. The times are simulated.
32 devices in a mesh: doc: 8 (over z, y), head: 4 (over x, core).
Axes of the slice: x: 2, y: 2, z: 4, core: 2. Of those that a mesh axis runs over, the one named last changes fastest.
Arguments:
- target_q: bfloat16 [1024, 2048], P('doc', 'head'), may hold values from -300 to 300
- target_kv: bfloat16 [1024, 512], P('doc', 'head'), may hold values from -8 to 8
- doc_kv: bfloat16 [8, 384, 512], P('doc', None, 'head'), may hold values from -6 to 6
- doc_lengths: int32 [8], replicated, may hold values from 1 to 384, 2304 in all
- segment_ids: int32 [1024], replicated, may hold values from 0 to 15, never falling along the last dimension, each value on 1 to 128 neighbouring positions
- out_weight: bfloat16 [2048, 8192], P('head', 'doc'), may hold values from -0.125 to 0.125
Outputs:
- projected: bfloat16 [1024, 8192], P('head', 'doc')
Inputs may be any that keep to these rules, and one draw needn't show every extreme that they name: `segment_ids`: segment numbers never fall along the target rows, and each segment spans at most 128 rows.
All inputs are finite; a program needn't handle non-finite values.
Results may differ from a plain program's by a relative error of at most 0.005.
Values may be sent and summed in bfloat16 or wider, within the bound.
A program may use at most 64 MiB of HBM per device.

v0:
```python
import math

import jax
import jax.numpy as jnp
from jax import lax
from jax.sharding import PartitionSpec as P

masked_score = -1e30


def swapped(array, axis, stride):
    return lax.ppermute(array, axis, [(i, i ^ 1 << stride) for i in range(lax.axis_size(axis))])


def passed_along(value, axis, steps):
    count = lax.axis_size(axis)
    initial, last = (max(0, -steps), min(count, count - steps))
    return lax.ppermute(value, axis, [(source, source + steps) for source in range(initial, last)])


def block_stats(queries, key_block, value_block, visible):
    scaling = 1.0 / math.sqrt(key_block.shape[1])
    scores = (
        lax.dot_general(
            queries, key_block, (((1,), (1,)), ((), ())), preferred_element_type=jnp.float32
        )
        * scaling
    )
    scores = jnp.where(visible, scores, masked_score)
    highest = jnp.max(scores, axis=1)
    weights = jnp.exp(scores - highest[:, None])
    summed = jnp.sum(weights, axis=1)
    blended = jnp.dot(weights.astype(jnp.bfloat16), value_block, preferred_element_type=jnp.float32)
    return (highest, summed, blended)


def merge_stats(state_now, incoming):
    highest = jnp.maximum(state_now[0], incoming[0])
    old_factor = jnp.exp(state_now[0] - highest)
    new_factor = jnp.exp(incoming[0] - highest)
    summed = state_now[1] * old_factor + incoming[1] * new_factor
    blended = state_now[2] * old_factor[:, None] + incoming[2] * new_factor[:, None]
    return (highest, summed, blended)


def body(target_q, target_kv, doc_kv, doc_lengths, segment_ids, out_weight):
    row_count = target_q.shape[0]
    head_dim = target_kv.shape[1]
    per_device = target_q.shape[1] // head_dim
    queries = target_q.reshape(row_count * per_device, head_dim)
    parity = lax.axis_index("head") % 2
    doc_index = lax.axis_index("doc")

    def arrange(own_part, partner):
        return (
            jnp.where(parity == 0, own_part, partner),
            jnp.where(parity == 0, partner, own_part),
        )

    initial = (
        jnp.full((queries.shape[0],), masked_score, jnp.float32),
        jnp.zeros((queries.shape[0],), jnp.float32),
        jnp.zeros((queries.shape[0], head_dim), jnp.float32),
    )
    partner_doc, partner_tgt = swapped((doc_kv, target_kv), "head", 0)
    doc_keys, doc_values = arrange(doc_kv, partner_doc)
    key_docs = lax.all_gather(doc_keys, "doc", axis=0, tiled=True)
    value_docs = lax.all_gather(doc_values, "doc", axis=0, tiled=True)
    slot_index = jnp.arange(key_docs.shape[1], dtype=jnp.int32)

    def attend_doc(doc_step, running):
        key_block = lax.dynamic_index_in_dim(key_docs, doc_step, 0, keepdims=False)
        value_block = lax.dynamic_index_in_dim(value_docs, doc_step, 0, keepdims=False)
        length = lax.dynamic_index_in_dim(doc_lengths, doc_step, 0, keepdims=False)
        visible = (slot_index < length)[None, :]
        return merge_stats(running, block_stats(queries, key_block, value_block, visible))

    stats = lax.fori_loop(0, key_docs.shape[0], attend_doc, initial)
    own_keys, own_values = arrange(target_kv, partner_tgt)
    prev_keys, prev_values = passed_along((own_keys, own_values), "doc", 1)
    own_seg = lax.dynamic_slice_in_dim(segment_ids, doc_index * row_count, row_count)
    prev_start = jnp.maximum(doc_index - 1, 0) * row_count
    prev_seg = jnp.where(
        doc_index > 0, lax.dynamic_slice_in_dim(segment_ids, prev_start, row_count), -1
    )
    token_pos = jnp.arange(row_count, dtype=jnp.int32)
    own_mask = (own_seg[:, None] == own_seg[None, :]) & (token_pos[None, :] <= token_pos[:, None])
    prev_mask = own_seg[:, None] == prev_seg[None, :]
    stats = merge_stats(
        stats, block_stats(queries, own_keys, own_values, jnp.repeat(own_mask, per_device, axis=0))
    )
    stats = merge_stats(
        stats,
        block_stats(queries, prev_keys, prev_values, jnp.repeat(prev_mask, per_device, axis=0)),
    )
    attention = (
        (stats[2] / stats[1][:, None])
        .astype(jnp.bfloat16)
        .reshape(row_count, per_device * head_dim)
    )
    gathered = lax.all_gather(attention, "doc", axis=0, tiled=True)
    result = lax.psum_scatter(
        jnp.dot(gathered, out_weight, preferred_element_type=jnp.float32),
        "head",
        scatter_dimension=0,
        tiled=True,
    )
    return result.astype(jnp.bfloat16)


def solution(mesh):
    placed = (
        P("doc", "head"),
        P("doc", "head"),
        P("doc", None, "head"),
        P(),
        P(),
        P("head", "doc"),
    )
    return jax.shard_map(
        body, mesh=mesh, in_specs=placed, out_specs=P("head", "doc"), check_vma=False
    )
```

profile of v0, /device:TPU:21, one launch (start us, length us, event | category | flops | bytes accessed | tf_op | source)
XLA Modules:
  0.0 205.7 jit_solution(15352952914273228183)
XLA Ops:
  6.5 0.7 collective-permute-start.1
  7.2 0.8 fusion.38
  8.3 0.1 copy.9
  8.5 0.1 copy.10
  8.6 1.0 reshape.30
  9.7 1.4 broadcast_select_fusion.3
  11.0 3.1 %collective-permute-start.2 = (bf16[128,128]{1,0:T(8,128)(2,1)S(1)}, bf16[128,128]{1,0:T(8,128)(2,1)S(1)}, u32[]{:S(2)}, u32[]{:S(2)}) collective-permute-start(bf16[128,128]{1,0:T(8,128)(2,1)S(1)} %get-tuple-element.222), channel_id=1, source_target_pairs={{0,4},{4,8},{8,12},{12,16},{16,20},{20,24},{24,28},{1,5},{5,9},{9,... | collective-permute-start | bytes 98312 | tf_op jit(solution)/shard_map/ppermute | solution.py:18
  14.2 3.1 %collective-permute-start.3 = (bf16[128,128]{1,0:T(8,128)(2,1)}, bf16[128,128]{1,0:T(8,128)(2,1)}, u32[]{:S(2)}, u32[]{:S(2)}) collective-permute-start(bf16[128,128]{1,0:T(8,128)(2,1)} %get-tuple-element.223), channel_id=1, source_target_pairs={{0,4},{4,8},{8,12},{12,16},{16,20},{20,24},{24,28},{1,5},{5,9},{9,... | collective-permute-start | bytes 98312 | tf_op jit(solution)/shard_map/ppermute | solution.py:18
  17.3 0.2 fusion.40
  17.5 0.6 fusion.24
  18.2 0.2 fusion.39
  18.4 0.6 fusion.26
  19.0 0.9 broadcast_select_fusion
  20.0 22.5 %all_gather.10 = bf16[8,384,128]{2,1,0:T(8,128)(2,1)S(1)} all-gather(bf16[1,384,128]{2,1,0:T(8,128)(2,1)S(1)} %get-tuple-element.220), channel_id=1, replica_groups=mesh['doc'=8,'head'=4] {'doc'}, dimensions={0}, use_global_device_ids=true | all-gather | bytes 884736 | tf_op jit(solution)/shard_map/all_gather | solution.py:68
  42.4 26.4 %all_gather.9 = bf16[8,384,128]{2,1,0:T(8,128)(2,1)S(1)} all-gather(bf16[1,384,128]{2,1,0:T(8,128)(2,1)S(1)} %get-tuple-element.221), channel_id=1, replica_groups=mesh['doc'=8,'head'=4] {'doc'}, dimensions={0}, use_global_device_ids=true | all-gather | bytes 884736 | tf_op jit(solution)/shard_map/all_gather | solution.py:67
  68.8 21.6 %while.18 = (s32[]{:T(128)}, f32[512]{0:T(512)S(1)}, f32[512]{0:T(512)S(1)}, f32[512,128]{1,0:T(8,128)S(1)}, s32[8]{0:T(128)}, /*index=5*/bf16[8,384,128]{2,1,0:...) while((s32[]{:T(128)}, f32[512]{0:T(512)S(1)}, ...), condition=%wide.region_3.4_spmd.clone, body=%wide.region_0.3_spmd.clone.sunk | while | flops 102305152 | bytes 3240976 | solution.py:78
  68.8 1.2 dynamic_slice.51
  70.0 0.6 iota_compare_fusion.3
  70.6 0.3 fusion.61
  70.9 0.2 fusion.62
  71.0 0.4 fusion.64
  71.5 1.2 dynamic_slice.51
  72.7 0.6 iota_compare_fusion.3
  73.3 0.3 fusion.61
  73.6 0.2 fusion.62
  73.7 0.4 fusion.64
  74.2 1.2 dynamic_slice.51
  75.4 0.6 iota_compare_fusion.3
  76.0 0.3 fusion.61
  76.3 0.2 fusion.62
  76.4 0.4 fusion.64
  76.9 1.2 dynamic_slice.51
  78.1 0.6 iota_compare_fusion.3
  78.7 0.3 fusion.61
  79.0 0.2 fusion.62
  79.2 0.4 fusion.64
  79.6 1.2 dynamic_slice.51
  80.8 0.6 iota_compare_fusion.3
  81.4 0.3 fusion.61
  81.7 0.2 fusion.62
  81.9 0.4 fusion.64
  82.3 1.2 dynamic_slice.51
  83.5 0.6 iota_compare_fusion.3
  84.1 0.3 fusion.61
  84.4 0.2 fusion.62
  84.6 0.4 fusion.64
  85.0 1.2 dynamic_slice.51
  86.3 0.6 iota_compare_fusion.3
  86.8 0.3 fusion.61
  87.1 0.2 fusion.62
  87.3 0.4 fusion.64
  87.7 1.2 dynamic_slice.51
  89.0 0.6 iota_compare_fusion.3
  89.5 0.3 fusion.61
  89.8 0.2 fusion.62
  90.0 0.4 fusion.64
  90.4 0.7 multiply_add_fusion
  91.1 1.0 convolution_multiply_fusion.2
  92.1 1.2 fusion.23
  93.3 0.7 reshape.33
  94.1 51.7 %all-gather.2.cloned.1.call-done = bf16[1024,512]{1,0:T(8,128)(2,1)} async-done(((bf16[128,512]{1,0:T(8,128)(2,1)}), bf16[1024,512]{1,0:T(8,128)(2,1)}) %all-gather.2.cloned.1.call-update) | async-done | bytes 1048592 | tf_op jit(solution)/shard_map/all_gather | solution.py:101
  145.8 4.4 %fusion.41 = f32[1024,1024]{1,0:T(8,128)} fusion(bf16[1024,512]{1,0:T(8,128)(2,1)} %all-gather.2.cloned.1.call-done, bf16[512,1024]{1,0:T(8,128)(2,1)S(1)} %copy-done), kind=kOutput, calls=%fused_computation.62 | convolution fusion | flops 1073741824 | bytes 6291456 | tf_op jit(solution)/shard_map/dot_general | solution.py:103
  150.3 46.5 %reduce-scatter.2.cloned.1.call-done = f32[256,1024]{1,0:T(8,128)} async-done(((f32[1024,1024]{1,0:T(8,128)}), f32[256,1024]{1,0:T(8,128)}) %reduce-scatter.2.cloned.1.call-update) | async-done | bytes 1048592 | tf_op jit(solution)/shard_map/reduce_scatter | solution.py:102
  196.7 2.1 %convert_element_type.20 = bf16[256,1024]{1,0:T(8,128)(2,1)} convert(f32[256,1024]{1,0:T(8,128)} %reduce-scatter.2.cloned.1.call-done) | non-fusion elementwise | flops 262144 | bytes 1572864 | tf_op jit(solution)/shard_map/convert_element_type | solution.py:108
  (25 shorter events, 0.5 us)
Async XLA Ops:
  6.5 139.3 %copy-start = (bf16[512,1024]{1,0:T(8,128)(2,1)S(1)}, bf16[512,1024]{1,0:T(8,128)(2,1)}, u32[]{:S(2)}) copy-start(bf16[512,1024]{1,0:T(8,128)(2,1)} %param.13) | copy-start | bytes 3145732
  6.5 139.3 %all-gather.2.cloned.1.call-start = ((), (), s32[]{:S(2)}) async-start(), calls=%async_computation.1 | async-start | bytes 1179648 | tf_op jit(solution)/shard_map/all_gather | solution.py:101
  6.5 3.1 %collective-permute-start.1 = (bf16[128,128]{1,0:T(8,128)(2,1)}, bf16[128,128]{1,0:T(8,128)(2,1)S(1)}, u32[]{:S(2)}, u32[]{:S(2)}) collective-permute-start(bf16[128,128]{1,0:T(8,128)(2,1)} %param.9), channel_id=1, source_target_pairs={{0,1},{1,0},{2,3},{3,2},{4,5},{5,4},{6,7},{7,6},{8,9},{9,8},{10,11... | collective-permute-start | bytes 98312 | tf_op jit(solution)/shard_map/ppermute | solution.py:12
  7.2 11.8 %collective-permute-start = (bf16[1,384,128]{2,1,0:T(8,128)(2,1)}, bf16[1,384,128]{2,1,0:T(8,128)(2,1)S(1)}, u32[]{:S(2)}, u32[]{:S(2)}) collective-permute-start(bf16[1,384,128]{2,1,0:T(8,128)(2,1)} %param.10), channel_id=1, source_target_pairs={{0,1},{1,0},{2,3},{3,2},{4,5},{5,4},{6,7},{7,6},{8,9},{9,8},{10,11... | collective-permute-start | bytes 294920 | tf_op jit(solution)/shard_map/ppermute | solution.py:12
  11.0 7.1 %collective-permute-start.2 = (bf16[128,128]{1,0:T(8,128)(2,1)S(1)}, bf16[128,128]{1,0:T(8,128)(2,1)S(1)}, u32[]{:S(2)}, u32[]{:S(2)}) collective-permute-start(bf16[128,128]{1,0:T(8,128)(2,1)S(1)} %get-tuple-element.222), channel_id=1, source_target_pairs={{0,4},{4,8},{8,12},{12,16},{16,20},{20,24},{24,28},{1,5},{5,9},{9,... | collective-permute-start | bytes 98312 | tf_op jit(solution)/shard_map/ppermute | solution.py:18
  14.2 76.9 %collective-permute-start.3 = (bf16[128,128]{1,0:T(8,128)(2,1)}, bf16[128,128]{1,0:T(8,128)(2,1)}, u32[]{:S(2)}, u32[]{:S(2)}) collective-permute-start(bf16[128,128]{1,0:T(8,128)(2,1)} %get-tuple-element.223), channel_id=1, source_target_pairs={{0,4},{4,8},{8,12},{12,16},{16,20},{20,24},{24,28},{1,5},{5,9},{9,... | collective-permute-start | bytes 98312 | tf_op jit(solution)/shard_map/ppermute | solution.py:18
  94.0 102.7 %reduce-scatter.2.cloned.1.call-start = ((), (), s32[]{:S(2)}) async-start(), calls=%async_computation.2 | async-start | bytes 5242880 | tf_op jit(solution)/shard_map/reduce_scatter | solution.py:102
Sparse Core Ops, SparseCore 0:
  94.2 51.6 all-gather.1
  150.4 46.2 reduce-scatter.1
where the time goes:
time: 208 us; the launch traced here: 206 us
  waiting for transfers between devices  98.2 us (47%)
  blocking collectives  48.8 us (23%)
  between operations  13.6 us (7%)
  other arithmetic  13.1 us (6%)
  matrix products  12.6 us (6%)
  local copies, waits for them, and re-layouts  12 us (6%)
  starting transfers between devices  7.01 us (3%)
    all_gather x1, waiting for transfers between devices, body(): gathered = lax.all_gather(attention, 'doc', axis=0, tiled=True)  51.7 us
    reduce_scatter x1, waiting for transfers between devices, body(): lax.psum_scatter(jnp.dot(gathered, out_weight, preferred_element_type=jnp...  46.5 us
    all_gather x1, blocking collectives, body(): key_docs = lax.all_gather(doc_keys, 'doc', axis=0, tiled=True)  26.4 us
    all_gather x1, blocking collectives, body(): value_docs = lax.all_gather(doc_values, 'doc', axis=0, tiled=True)  22.5 us
    dynamic_slice x8, local copies, waits for them, and re-layouts, attend_doc(): length = lax.dynamic_index_in_dim(doc_lengths, doc_step, 0, keepdims=False)  9.87 us
    ppermute x2, starting transfers between devices, passed_along(): lax.ppermute(value, axis, [(source, source + steps) for source in range(i...  6.29 us
    dot_general x10, matrix products, block_stats(): jnp.dot(weights.astype(jnp.bfloat16), value_block, preferred_element_type...  5.51 us
    lt x8, other arithmetic, attend_doc(): visible = (slot_index < length)[None, :]  4.5 us
  transfers between devices with their start and end apart: 6, of which 2 were waited for; matrix products, arithmetic and copies ran while one was open for 14% of the time, Pallas kernels for 0%

commit v1 on v0

v1 whole, which is shorter than its diff:
```python
import math

import jax
import jax.numpy as jnp
from jax import lax
from jax.experimental import pallas as pl
from jax.experimental.pallas import tpu as pltpu
from jax.sharding import PartitionSpec as P

MASKED = -1e30
F32 = jnp.float32
BF16 = jnp.bfloat16


def ordered(pos, count, k):
    right = count - 1 - pos
    both = jnp.minimum(pos, right)
    near = jnp.where(k % 2 == 1, (k + 1) // 2, -(k // 2))
    far = jnp.where(right > pos, k - both, both - k)
    return pos + jnp.where(k <= 2 * both, near, far)


def kernel(
    ndoc,
    nhead,
    q_ref,
    tkv_ref,
    dkv_ref,
    len_ref,
    seg_ref,
    w_ref,
    out_ref,
    kv,
    tkv,
    wbuf,
    qbuf,
    m_s,
    l_s,
    acc_s,
    att,
    abuf,
    own,
    sbuf,
    rbuf,
    s_z,
    s_y,
    s_sib,
    r_doc,
    r_sib,
    s_t,
    r_t,
    s_w,
    r_w,
    l_w,
    s_a,
    s_az,
    s_ay,
    r_a,
    s_p,
    r_p,
):
    rows = q_ref.shape[0]
    hd = tkv_ref.shape[1]
    heads = q_ref.shape[1] // hd
    cols = q_ref.shape[1]
    Z = ndoc // 2
    PAIRS = nhead // 2
    me = lax.axis_index("doc")
    hi = lax.axis_index("head")
    zi, y = me // 2, me % 2
    p, c = hi // 2, hi % 2
    sib = 2 * p + 1 - c
    ynb = 2 * zi + 1 - y
    t = zi % 2
    owner = 2 * p + t
    has_l, has_r = zi > 0, zi < Z - 1
    has_prev, has_next = me > 0, me < ndoc - 1
    coef = math.log2(math.e) / math.sqrt(hd)

    def rc(src, dst, ss, rs, doc, head):
        return pltpu.make_async_remote_copy(
            src_ref=src,
            dst_ref=dst,
            send_sem=ss,
            recv_sem=rs,
            device_id={"doc": doc, "head": head},
            device_id_type=pl.DeviceIdType.MESH,
        )

    barrier = pltpu.get_barrier_semaphore()

    def greet(doc, head):
        pl.semaphore_signal(
            barrier, inc=1, device_id={"doc": doc, "head": head}, device_id_type=pl.DeviceIdType.MESH
        )

    diag = jnp.where(y == 1, me + 1, me - 1)
    has_diag = ((y == 1) & has_r) | ((y == 0) & has_l)
    greet(me, sib)
    for core in range(2):
        greet(ynb, 2 * p + core)

        @pl.when(has_l)
        def _():
            greet(me - 2, 2 * p + core)

        @pl.when(has_r)
        def _():
            greet(me + 2, 2 * p + core)

        @pl.when(has_diag)
        def _():
            greet(diag, 2 * p + core)

    for k in range(1, PAIRS):
        greet(me, 2 * ((p + k) % PAIRS) + c)
    sides = sum(cond.astype(jnp.int32) for cond in (has_l, has_r, has_diag))
    pl.semaphore_wait(barrier, 2 + PAIRS + 2 * sides)

    def send_r(src, doc):
        return rc(src, kv.at[c, doc], s_z.at[doc], r_doc.at[doc], me + 2, hi)

    def send_l(src, doc):
        return rc(src, kv.at[c, doc], s_z.at[doc], r_doc.at[doc], me - 2, hi)

    s_l0 = s_w.at[1]

    def send_l0(src, doc):
        return rc(src, kv.at[c, doc], s_l0, r_doc.at[doc], me - 2, hi)

    def send_y(src, doc):
        return rc(src, kv.at[c, doc], s_y.at[doc], r_doc.at[doc], ynb, hi)

    def send_sib(src, doc):
        return rc(src, kv.at[c, doc], s_sib.at[doc], r_sib.at[doc], me, sib)

    own_block = dkv_ref.at[0]
    t_own = rc(tkv_ref, tkv.at[c, pl.ds(rows, rows)], s_t.at[0], r_t.at[1], me, sib)
    t_next = [
        rc(tkv_ref, tkv.at[c, pl.ds(0, rows)], s_t.at[1], r_t.at[2], me + 1, hi),
        rc(tkv_ref, tkv.at[c, pl.ds(0, rows)], s_t.at[2], r_t.at[0], me + 1, sib),
    ]
    t_own.start()
    pl.when(has_r)(lambda: send_r(own_block, me).start())
    pl.when(has_l)(lambda: send_l0(own_block, me).start())
    send_y(own_block, me).start()
    send_sib(own_block, me).start()

    @pl.when(has_next)
    def _():
        t_next[0].start()
        t_next[1].start()

    w_local = pltpu.make_async_copy(w_ref, wbuf.at[c], l_w)
    w_remote = rc(w_ref, wbuf.at[c], s_w.at[0], r_w, me, sib)
    w_local.start()
    w_remote.start()

    kv[c, me] = dkv_ref[0]
    tkv[c, pl.ds(rows, rows)] = tkv_ref[...]
    for j in range(heads):
        qbuf[j * rows : (j + 1) * rows] = q_ref[:, j * hd : (j + 1) * hd]

    @pl.when(me == 0)
    def _():
        tkv[:, pl.ds(0, rows)] = jnp.zeros((2, rows, hd), BF16)

    def attend(keys, values, mask_of, first):
        half = cols // 2
        for part in range(2):
            at = slice(part * half, (part + 1) * half)
            scores = lax.dot_general(
                keys, qbuf[at], (((1,), (1,)), ((), ())), preferred_element_type=F32
            )
            scores = jnp.where(mask_of(half), scores, MASKED)
            high = jnp.max(scores, axis=0, keepdims=True)
            if not first:
                before = m_s[:, at]
                high = jnp.maximum(high, before)
            weights = jnp.exp2((scores - high) * coef)
            total = jnp.sum(weights, axis=0, keepdims=True)
            blended = lax.dot_general(
                values,
                weights.astype(BF16),
                (((0,), (0,)), ((), ())),
                preferred_element_type=F32,
            )
            if not first:
                factor = jnp.exp2((before - high) * coef)
                total = total + factor * l_s[:, at]
                blended = blended + factor * acc_s[:, at]
            m_s[:, at] = high
            l_s[:, at] = total
            acc_s[:, at] = blended

    own_row = seg_ref[pl.ds(me, 1), :]
    prev_row = seg_ref[pl.ds(jnp.maximum(me - 1, 0), 1), :]

    def column(row):
        return jnp.broadcast_to(row.astype(F32), (rows, rows)).T

    own_col, prev_col = column(own_row), column(prev_row)
    own_rowf = jnp.broadcast_to(own_row.astype(F32), (rows, rows))
    key_pos = lax.broadcasted_iota(jnp.int32, (rows, rows), 0)
    row_pos = lax.broadcasted_iota(jnp.int32, (rows, rows), 1)
    prev_mask = jnp.where(has_prev, (prev_col == own_rowf).astype(F32), 0.0)
    own_mask = jnp.where((own_col == own_rowf) & (key_pos <= row_pos), 1.0, 0.0)
    tmask = jnp.concatenate([prev_mask, own_mask], axis=0)

    t_own.wait_recv()

    @pl.when(has_prev)
    def _():
        t_next[0].wait_recv()
        t_next[1].wait_recv()

    attend(
        tkv[0],
        tkv[1],
        lambda n: jnp.concatenate([tmask] * (n // rows), axis=1) > 0.5,
        True,
    )

    def attend_doc(doc):
        send_sib(own_block, doc).wait_recv()
        keys = kv[0, doc]
        length = len_ref[doc]

        def mask_of(n):
            return lax.broadcasted_iota(jnp.int32, (keys.shape[0], n), 0) < length

        attend(keys, kv[1, doc], mask_of, False)

    def doc_step(i, _):
        @pl.when(i < Z)
        def _():
            z = ordered(zi, Z, i)
            doc = 2 * z + y
            block = kv.at[c, doc]
            send_y(own_block, doc).wait_recv()
            pl.when((z < zi) & has_r)(lambda: send_r(block, doc).start())
            pl.when((z > zi) & has_l)(lambda: send_l(block, doc).start())
            send_y(block, doc).start()
            send_sib(block, doc).start()

        z = ordered(zi, Z, i - 1)
        other = 2 * z + 1 - y
        send_y(own_block, other).wait_recv()
        send_sib(kv.at[c, other], other).start()
        attend_doc(2 * z + y)
        attend_doc(other)
        return 0

    lax.fori_loop(1, Z + 1, doc_step, 0)

    for j in range(heads):
        at = slice(j * rows, (j + 1) * rows)
        att[:, at] = (acc_s[:, at] / l_s[:, at]).T.astype(BF16)

    def unit(z, yy, half):
        return abuf.at[z // 2, yy, half]

    a_sib = rc(att, unit(zi, y, c), s_a.at[0], r_a.at[zi // 2, y, c], me, sib)
    a_r = rc(att, unit(zi, y, c), s_a.at[1], r_a.at[zi // 2, y, c], me + 2, owner)
    a_l = rc(att, unit(zi, y, c), s_a.at[2], r_a.at[zi // 2, y, c], me - 2, owner)
    a_y = rc(att, unit(zi, y, c), s_a.at[3], r_a.at[zi // 2, y, c], ynb, owner)
    pl.when(has_r)(lambda: a_r.start())
    pl.when(has_l)(lambda: a_l.start())
    a_y.start()
    pl.when(t != c)(lambda: a_sib.start())

    @pl.when(t == c)
    def _():
        abuf[zi // 2, y, c] = att[...]

    w_local.wait()
    w_remote.wait_recv()

    def fwd(z, half, doc, sems):
        return rc(
            unit(z, y, half),
            unit(z, y, half),
            sems.at[z // 2, half],
            r_a.at[z // 2, y, half],
            doc,
            hi,
        )

    def arrived(z, yy, half):
        rc(
            unit(z, yy, half), unit(z, yy, half), s_a.at[0], r_a.at[z // 2, yy, half], ynb, hi
        ).wait_recv()

    def part_copy(z, yy):
        return rc(sbuf.at[z // 2, yy], rbuf.at[p, yy], s_p.at[z // 2, yy], r_p.at[p, yy], me, z)

    def project(z, yy):
        part = jnp.dot(abuf[z // 2, yy, 0], wbuf[0], preferred_element_type=F32)
        part = part + jnp.dot(abuf[z // 2, yy, 1], wbuf[1], preferred_element_type=F32)

        @pl.when(z // 2 == p)
        def _():
            own[yy] = part

        @pl.when(z // 2 != p)
        def _():
            sbuf[z // 2, yy] = part.astype(BF16)
            part_copy(z, yy).start()

    def place(k):
        return 2 * ordered(zi // 2, Z // 2, k) + c

    def proj_step(k, _):
        @pl.when(k < Z // 2)
        def _():
            z = place(k)

            @pl.when(z == zi)
            def _():
                arrived(z, y, 1 - c)

            for half in range(2):

                @pl.when(z != zi)
                def _():
                    arrived(z, y, half)
                    fwd(z, half, ynb, s_ay).start()

                pl.when((z < zi) & has_r)(lambda: fwd(z, half, me + 2, s_az).start())
                pl.when((z > zi) & has_l)(lambda: fwd(z, half, me - 2, s_az).start())
            project(z, y)

        @pl.when(k > 0)
        def _():
            z = place(k - 1)
            arrived(z, 1 - y, 0)
            arrived(z, 1 - y, 1)
            project(z, 1 - y)

        return 0

    lax.fori_loop(0, Z // 2 + 1, proj_step, 0)

    def add_in(k, _):
        src = (p + k) % PAIRS
        for yy in range(2):
            rc(sbuf.at[src, yy], rbuf.at[src, yy], s_p.at[src, yy], r_p.at[src, yy], me, hi_of(src)).wait_recv()
            own[yy] = own[yy] + rbuf[src, yy].astype(F32)
        return 0

    def hi_of(src):
        return 2 * src + c

    if PAIRS == 2:
        src = 1 - p
        for yy in range(2):
            rc(sbuf.at[src, yy], rbuf.at[src, yy], s_p.at[src, yy], r_p.at[src, yy], me, hi_of(src)).wait_recv()
            out_ref[yy * rows : (yy + 1) * rows] = (own[yy] + rbuf[src, yy].astype(F32)).astype(BF16)
    else:
        lax.fori_loop(1, PAIRS, add_in, 0)
        for yy in range(2):
            out_ref[yy * rows : (yy + 1) * rows] = own[yy].astype(BF16)

    t_own.wait_send()

    @pl.when(has_next)
    def _():
        t_next[0].wait_send()
        t_next[1].wait_send()

    pl.when(has_r)(lambda: send_r(own_block, me).wait_send())
    pl.when(has_l)(lambda: send_l0(own_block, me).wait_send())
    w_remote.wait_send()

    def drain(z, _):
        doc = 2 * z + y
        send_y(own_block, doc).wait_send()
        send_sib(own_block, doc).wait_send()
        send_sib(own_block, 2 * z + 1 - y).wait_send()
        pl.when((z < zi) & has_r)(lambda: send_r(own_block, doc).wait_send())
        pl.when((z > zi) & has_l)(lambda: send_l(own_block, doc).wait_send())

        @pl.when(z % 2 == c)
        def _():
            for half in range(2):
                pl.when(z != zi)(lambda: fwd(z, half, ynb, s_ay).wait_send())
                pl.when((z < zi) & has_r)(lambda: fwd(z, half, me + 2, s_az).wait_send())
                pl.when((z > zi) & has_l)(lambda: fwd(z, half, me - 2, s_az).wait_send())

            @pl.when(z // 2 != p)
            def _():
                for yy in range(2):
                    part_copy(z, yy).wait_send()

        return 0

    lax.fori_loop(0, Z, drain, 0)
    pl.when(has_r)(lambda: a_r.wait_send())
    pl.when(has_l)(lambda: a_l.wait_send())
    a_y.wait_send()
    pl.when(t != c)(lambda: a_sib.wait_send())


def body(target_q, target_kv, doc_kv, doc_lengths, segment_ids, out_weight, ndoc, nhead):
    rows, cols = target_q.shape
    hd = target_kv.shape[1]
    slots = doc_kv.shape[1]
    wide = out_weight.shape[1]
    Z, pairs = ndoc // 2, nhead // 2
    vmem = pl.BlockSpec(memory_space=pltpu.VMEM)
    dma = pltpu.SemaphoreType.DMA
    flops = 4 * rows * cols * (ndoc * slots + 2 * rows) + 2 * ndoc * rows * cols * wide
    return pl.pallas_call(
        lambda *refs: kernel(ndoc, nhead, *refs),
        out_shape=jax.ShapeDtypeStruct((2 * rows, wide), BF16),
        in_specs=[
            vmem,
            vmem,
            vmem,
            pl.BlockSpec(memory_space=pltpu.SMEM),
            vmem,
            pl.BlockSpec(memory_space=pl.ANY),
        ],
        out_specs=vmem,
        scratch_shapes=[
            pltpu.VMEM((2, ndoc, slots, hd), BF16),
            pltpu.VMEM((2, 2 * rows, hd), BF16),
            pltpu.VMEM((2, cols, wide), BF16),
            pltpu.VMEM((cols // hd * rows, hd), BF16),
            pltpu.VMEM((1, cols // hd * rows), F32),
            pltpu.VMEM((1, cols // hd * rows), F32),
            pltpu.VMEM((hd, cols // hd * rows), F32),
            pltpu.VMEM((rows, cols), BF16),
            pltpu.VMEM((Z // 2, 2, 2, rows, cols), BF16),
            pltpu.VMEM((2, rows, wide), F32),
            pltpu.VMEM((pairs, 2, rows, wide), BF16),
            pltpu.VMEM((pairs, 2, rows, wide), BF16),
            dma((ndoc,)),
            dma((ndoc,)),
            dma((ndoc,)),
            dma((ndoc,)),
            dma((ndoc,)),
            dma((3,)),
            dma((3,)),
            dma((2,)),
            dma,
            dma,
            dma((4,)),
            dma((Z // 2, 2)),
            dma((Z // 2, 2)),
            dma((Z // 2, 2, 2)),
            dma((pairs, 2)),
            dma((pairs, 2)),
        ],
        compiler_params=pltpu.CompilerParams(
            collective_id=0, has_side_effects=True, vmem_limit_bytes=40 * 1024 * 1024
        ),
        cost_estimate=pl.CostEstimate(flops=flops, bytes_accessed=4 << 20, transcendentals=0),
    )(
        target_q,
        target_kv,
        doc_kv,
        doc_lengths,
        segment_ids.reshape(ndoc, rows),
        out_weight,
    )


def solution(mesh):
    ndoc, nhead = mesh.shape["doc"], mesh.shape["head"]
    placed = (
        P("doc", "head"),
        P("doc", "head"),
        P("doc", None, "head"),
        P(),
        P(),
        P("head", "doc"),
    )
    return jax.shard_map(
        lambda *args: body(*args, ndoc, nhead),
        mesh=mesh,
        in_specs=placed,
        out_specs=P("head", "doc"),
        check_vma=False,
    )
```

time: 208 us -> 57.2 us (0.28)
  the two profiles are of different devices: /device:TPU:21 before, /device:TPU:3 now
where the time goes in v1:
time: 57.2 us; the launch traced here: 56.9 us
  Pallas kernels  51 us (89%)
  local copies, waits for them, and re-layouts  5.91 us (10%)
    pallas_call x1, Pallas kernels, body(): pl.pallas_call(lambda *refs: kernel(ndoc, nhead, *refs), out_shape=jax.Sh...  51 us
    unnamed x13, local copies, waits for them, and re-layouts  5.91 us

profile of v1, /device:TPU:3, one launch (start us, length us, event | category | flops | bytes accessed | tf_op | source)
XLA Modules:
  0.0 56.9 jit_solution(5551683715238808795)
XLA Ops:
  0.0 0.0 copy-start.5
  0.0 0.7 %copy-done.5 = s32[8]{0:T(128)S(1)} copy-done((s32[8]{0:T(128)S(1)}, s32[8]{0:T(128)}, u32[]{:S(2)}) %copy-start.5) | copy-done | bytes 56
  0.7 0.0 copy-start
  0.7 1.2 %copy-done = bf16[512,1024]{1,0:T(8,128)(2,1)S(1)} copy-done((bf16[512,1024]{1,0:T(8,128)(2,1)S(1)}, bf16[512,1024]{1,0:T(8,128)(2,1)}, u32[]{:S(2)}) %copy-start) | copy-done | bytes 1048600
  1.9 0.0 copy-start.1
  1.9 0.9 %copy-done.1 = bf16[128,512]{1,0:T(8,128)(2,1)S(1)} copy-done((bf16[128,512]{1,0:T(8,128)(2,1)S(1)}, bf16[128,512]{1,0:T(8,128)(2,1)}, u32[]{:S(2)}) %copy-start.1) | copy-done | bytes 131096
  2.8 0.0 copy-start.2
  2.8 0.9 %copy-done.2 = bf16[1,384,128]{2,1,0:T(8,128)(2,1)S(1)} copy-done((bf16[1,384,128]{2,1,0:T(8,128)(2,1)S(1)}, bf16[1,384,128]{2,1,0:T(8,128)(2,1)}, u32[]{:S(2)}) %copy-start.2) | copy-done | bytes 98328
  3.7 0.0 copy-start.3
  3.7 0.8 %copy-done.3 = bf16[128,128]{1,0:T(8,128)(2,1)S(1)} copy-done((bf16[128,128]{1,0:T(8,128)(2,1)S(1)}, bf16[128,128]{1,0:T(8,128)(2,1)}, u32[]{:S(2)}) %copy-start.3) | copy-done | bytes 32792
  4.4 0.0 copy-start.4
  4.4 0.7 %copy-done.4 = s32[1024]{0:T(1024)S(1)} copy-done((s32[1024]{0:T(1024)S(1)}, s32[1024]{0:T(1024)}, u32[]{:S(2)}) %copy-start.4) | copy-done | bytes 4120
  5.1 51.0 %shard_map.64 = bf16[256,1024]{1,0:T(8,128)(2,1)S(1)} custom-call(bf16[128,512]{1,0:T(8,128)(2,1)S(1)} %copy-done.1, bf16[128,128]{1,0:T(8,128)(2,1)S(1)} %copy-done.3, bf16[1,384,128]{2,1,0:T(8,128)(2,1)S(1)} %copy-done.2, s32[8]{0:T(128)S(1)} %copy-done.5, s32[8,128]{1,0:T(8,128)S(1)} %bitcast.1, bf16[512,1024]{1,0:T(8,128)(2,1)S(1)} %copy-done), custom_call_target="tpu_custom_call" | custom-call | flops 1946157056 | bytes 4194304 | tf_op jit(solution)/shard_map/pallas_call | solution.py:413
  56.1 0.8 %copy.8 = bf16[256,1024]{1,0:T(8,128)(2,1)} copy(bf16[256,1024]{1,0:T(8,128)(2,1)S(1)} %shard_map.64) | data formatting | bytes 1048576
Async XLA Ops:
  0.0 0.7 %copy-start.5 = (s32[8]{0:T(128)S(1)}, s32[8]{0:T(128)}, u32[]{:S(2)}) copy-start(s32[8]{0:T(128)} %refs_3_.1) | copy-start | bytes 100
  0.7 1.2 %copy-start = (bf16[512,1024]{1,0:T(8,128)(2,1)S(1)}, bf16[512,1024]{1,0:T(8,128)(2,1)}, u32[]{:S(2)}) copy-start(bf16[512,1024]{1,0:T(8,128)(2,1)} %refs_5_.1) | copy-start | bytes 3145732
  1.9 0.9 %copy-start.1 = (bf16[128,512]{1,0:T(8,128)(2,1)S(1)}, bf16[128,512]{1,0:T(8,128)(2,1)}, u32[]{:S(2)}) copy-start(bf16[128,512]{1,0:T(8,128)(2,1)} %refs_0_.1) | copy-start | bytes 393220
  2.8 0.9 %copy-start.2 = (bf16[1,384,128]{2,1,0:T(8,128)(2,1)S(1)}, bf16[1,384,128]{2,1,0:T(8,128)(2,1)}, u32[]{:S(2)}) copy-start(bf16[1,384,128]{2,1,0:T(8,128)(2,1)} %refs_2_.1) | copy-start | bytes 294916
  3.7 0.8 %copy-start.3 = (bf16[128,128]{1,0:T(8,128)(2,1)S(1)}, bf16[128,128]{1,0:T(8,128)(2,1)}, u32[]{:S(2)}) copy-start(bf16[128,128]{1,0:T(8,128)(2,1)} %refs_1_.1) | copy-start | bytes 98308
  4.4 0.7 %copy-start.4 = (s32[1024]{0:T(1024)S(1)}, s32[1024]{0:T(1024)}, u32[]{:S(2)}) copy-start(s32[1024]{0:T(1024)} %param.10) | copy-start | bytes 12292

commit v2 on v1

v2 whole, which is shorter than its diff:
```python
import math

import jax
import jax.numpy as jnp
from jax import lax
from jax.experimental import pallas as pl
from jax.experimental.pallas import tpu as pltpu
from jax.sharding import PartitionSpec as P

MASKED = -1e30
F32 = jnp.float32
BF16 = jnp.bfloat16


def ordered(pos, count, k):
    right = count - 1 - pos
    both = jnp.minimum(pos, right)
    near = jnp.where(k % 2 == 1, (k + 1) // 2, -(k // 2))
    far = jnp.where(right > pos, k - both, both - k)
    return pos + jnp.where(k <= 2 * both, near, far)


def kernel(
    ndoc,
    nhead,
    q_in,
    tkv_in,
    dkv_in,
    len_in,
    seg_in,
    w_ref,
    out_ref,
    len_ref,
    seg_ref,
    s_in,
    kv,
    tkv,
    wbuf,
    qbuf,
    m_s,
    l_s,
    acc_s,
    att,
    abuf,
    own,
    sbuf,
    rbuf,
    s_z,
    s_y,
    s_sib,
    r_doc,
    r_sib,
    s_t,
    r_t,
    s_w,
    r_w,
    l_w,
    s_a,
    s_az,
    s_ay,
    r_a,
    s_p,
    r_p,
):
    rows, cols = q_in.shape
    hd = tkv_in.shape[1]
    heads = cols // hd
    Z = ndoc // 2
    PAIRS = nhead // 2
    me = lax.axis_index("doc")
    hi = lax.axis_index("head")
    zi, y = me // 2, me % 2
    p, c = hi // 2, hi % 2
    sib = 2 * p + 1 - c
    ynb = 2 * zi + 1 - y
    t = zi % 2
    owner = 2 * p + t
    has_prev, has_next = me > 0, me < ndoc - 1
    coef = math.log2(math.e) / math.sqrt(hd)

    def rc(src, dst, ss, rs, doc, head):
        return pltpu.make_async_remote_copy(
            src_ref=src,
            dst_ref=dst,
            send_sem=ss,
            recv_sem=rs,
            device_id={"doc": doc, "head": head},
            device_id_type=pl.DeviceIdType.MESH,
        )

    load_doc = pltpu.make_async_copy(dkv_in.at[0], kv.at[c, me], s_in.at[0])
    load_tgt = pltpu.make_async_copy(tkv_in, tkv.at[c, pl.ds(rows, rows)], s_in.at[1])
    loads = [
        pltpu.make_async_copy(
            q_in.at[:, pl.ds(j * hd, hd)], qbuf.at[pl.ds(j * rows, rows)], s_in.at[4 + j]
        )
        for j in range(heads)
    ]
    loads.append(pltpu.make_async_copy(len_in, len_ref, s_in.at[2]))
    loads.append(pltpu.make_async_copy(seg_in, seg_ref, s_in.at[3]))
    w_local = pltpu.make_async_copy(w_ref, wbuf.at[c], l_w)
    for load in [load_doc, load_tgt] + loads + [w_local]:
        load.start()

    barrier = pltpu.get_barrier_semaphore()

    def greet(doc, head):
        pl.semaphore_signal(
            barrier, inc=1, device_id={"doc": doc, "head": head}, device_id_type=pl.DeviceIdType.MESH
        )

    diag = jnp.where(y == 1, me + 1, me - 1)
    has_diag = ((y == 1) & has_next) | ((y == 0) & has_prev)
    greet(me, sib)
    for core in range(2):
        greet(ynb, 2 * p + core)

        for k in range(1, Z):
            greet(2 * ((zi + k) % Z) + y, 2 * p + core)

        @pl.when(has_diag)
        def _():
            greet(diag, 2 * p + core)

    for k in range(1, PAIRS):
        greet(me, 2 * ((p + k) % PAIRS) + c)
    pl.semaphore_wait(barrier, 2 * Z + PAIRS + 2 * has_diag.astype(jnp.int32))

    def send_z(z):
        return rc(own_block, kv.at[c, me], s_z.at[z], r_doc.at[me], 2 * z + y, hi)

    def at_distance(k, act):
        pl.when(zi + k < Z)(lambda: act(zi + k))
        pl.when(zi - k >= 0)(lambda: act(zi - k))

    def advance(k, copy):
        at_distance(k, lambda z: copy(z).wait_send())
        at_distance(k + 1, lambda z: copy(z).start())

    def send_y(src, doc):
        return rc(src, kv.at[c, doc], s_y.at[doc], r_doc.at[doc], ynb, hi)

    def send_sib(src, doc):
        return rc(src, kv.at[c, doc], s_sib.at[doc], r_sib.at[doc], me, sib)

    own_block, tkv_ref = kv.at[c, me], tkv.at[c, pl.ds(rows, rows)]
    load_doc.wait()
    load_tgt.wait()
    t_own = rc(tkv_ref, tkv.at[c, pl.ds(rows, rows)], s_t.at[0], r_t.at[1], me, sib)
    t_next = [
        rc(tkv_ref, tkv.at[c, pl.ds(0, rows)], s_t.at[1], r_t.at[2], me + 1, hi),
        rc(tkv_ref, tkv.at[c, pl.ds(0, rows)], s_t.at[2], r_t.at[0], me + 1, sib),
    ]
    send_y(own_block, me).start()
    at_distance(1, lambda z: send_z(z).start())
    send_sib(own_block, me).start()
    t_own.start()

    @pl.when(has_next)
    def _():
        t_next[0].start()
        t_next[1].start()

    w_remote = rc(w_ref, wbuf.at[c], s_w, r_w, me, sib)
    w_remote.start()

    @pl.when(me == 0)
    def _():
        tkv[:, pl.ds(0, rows)] = jnp.zeros((2, rows, hd), BF16)

    def attend(keys, values, mask_of):
        half = cols // 2
        for part in range(2):
            at = slice(part * half, (part + 1) * half)
            scores = lax.dot_general(
                keys, qbuf[at], (((1,), (1,)), ((), ())), preferred_element_type=F32
            )
            scores = jnp.where(mask_of(half), scores, MASKED)
            before = m_s[:, at]
            high = jnp.maximum(jnp.max(scores, axis=0, keepdims=True), before)
            weights = jnp.exp2((scores - high) * coef)
            blended = lax.dot_general(
                values,
                weights.astype(BF16),
                (((0,), (0,)), ((), ())),
                preferred_element_type=F32,
            )
            factor = jnp.exp2((before - high) * coef)
            m_s[:, at] = high
            l_s[:, at] = jnp.sum(weights, axis=0, keepdims=True) + factor * l_s[:, at]
            acc_s[:, at] = blended + factor * acc_s[:, at]

    for load in loads:
        load.wait()
    m_s[...] = jnp.full_like(m_s, MASKED)
    l_s[...] = jnp.zeros_like(l_s)
    acc_s[...] = jnp.zeros_like(acc_s)

    def attend_doc(doc):
        send_sib(own_block, doc).wait_recv()
        keys = kv[0, doc]
        length = len_ref[doc]

        def mask_of(n):
            return lax.broadcasted_iota(jnp.int32, (keys.shape[0], n), 0) < length

        attend(keys, kv[1, doc], mask_of)

    def own_step(i, _):
        @pl.when(i < Z)
        def _():
            advance(i, send_z)
            z = ordered(zi, Z, i)
            doc = 2 * z + y
            block = kv.at[c, doc]
            send_y(own_block, doc).wait_recv()
            send_y(block, doc).start()
            send_sib(block, doc).start()

        attend_doc(2 * ordered(zi, Z, i - 1) + y)
        return 0

    def other_step(i, _):
        @pl.when(i < Z)
        def _():
            doc = 2 * ordered(zi, Z, i) + 1 - y
            send_y(own_block, doc).wait_recv()
            send_sib(kv.at[c, doc], doc).start()

        @pl.when(i > 0)
        def _():
            attend_doc(2 * ordered(zi, Z, i - 1) + 1 - y)

        return 0

    lax.fori_loop(1, Z + 1, own_step, 0)

    own_row = seg_ref[pl.ds(me, 1), :]
    prev_row = seg_ref[pl.ds(jnp.maximum(me - 1, 0), 1), :]

    def column(row):
        return jnp.broadcast_to(row.astype(F32), (rows, rows)).T

    own_col, prev_col = column(own_row), column(prev_row)
    own_rowf = jnp.broadcast_to(own_row.astype(F32), (rows, rows))
    key_pos = lax.broadcasted_iota(jnp.int32, (rows, rows), 0)
    row_pos = lax.broadcasted_iota(jnp.int32, (rows, rows), 1)
    prev_mask = jnp.where(has_prev, (prev_col == own_rowf).astype(F32), 0.0)
    own_mask = jnp.where((own_col == own_rowf) & (key_pos <= row_pos), 1.0, 0.0)
    tmask = jnp.concatenate([prev_mask, own_mask], axis=0)

    t_own.wait_recv()

    @pl.when(has_prev)
    def _():
        t_next[0].wait_recv()
        t_next[1].wait_recv()

    attend(
        tkv[0],
        tkv[1],
        lambda n: jnp.concatenate([tmask] * (n // rows), axis=1) > 0.5,
    )

    lax.fori_loop(0, Z + 1, other_step, 0)

    for j in range(heads):
        at = slice(j * rows, (j + 1) * rows)
        att[:, at] = (acc_s[:, at] / l_s[:, at]).T.astype(BF16)

    def unit(z, yy, half):
        return abuf.at[z // 2, yy, half]

    a_sib = rc(att, unit(zi, y, c), s_a.at[0], r_a.at[zi // 2, y, c], me, sib)

    def a_z(z):
        return rc(att, unit(zi, y, c), s_az.at[z], r_a.at[zi // 2, y, c], 2 * z + y, owner)

    a_y = rc(att, unit(zi, y, c), s_a.at[1], r_a.at[zi // 2, y, c], ynb, owner)
    a_y.start()
    for k in range(Z - 1, 0, -1):
        at_distance(k, lambda z: a_z(z).start())
    pl.when(t != c)(lambda: a_sib.start())

    @pl.when(t == c)
    def _():
        abuf[zi // 2, y, c] = att[...]

    w_local.wait()
    w_remote.wait_recv()

    def fwd(z, half):
        block = unit(z, y, half)
        return rc(block, block, s_ay.at[z // 2, half], r_a.at[z // 2, y, half], ynb, hi)

    def arrived(z, yy, half):
        rc(
            unit(z, yy, half), unit(z, yy, half), s_a.at[0], r_a.at[z // 2, yy, half], ynb, hi
        ).wait_recv()

    def part_copy(z, yy):
        return rc(sbuf.at[z // 2, yy], rbuf.at[p, yy], s_p.at[z // 2, yy], r_p.at[p, yy], me, z)

    def project(z, yy):
        part = jnp.dot(abuf[z // 2, yy, 0], wbuf[0], preferred_element_type=F32)
        part = part + jnp.dot(abuf[z // 2, yy, 1], wbuf[1], preferred_element_type=F32)
        sbuf[z // 2, yy] = part.astype(BF16)
        part_copy(z, yy).start()

    def place(k):
        return 2 * ordered(zi // 2, Z // 2, k) + c

    def own_rows(k, _):
        z = 2 * ((p + 1 + k) % PAIRS) + c

        @pl.when(z == zi)
        def _():
            arrived(z, y, 1 - c)

        for half in range(2):

            @pl.when(z != zi)
            def _():
                arrived(z, y, half)
                fwd(z, half).start()

        pl.when(z // 2 != p)(lambda: project(z, y))
        return 0

    def other_rows(k, _):
        z = 2 * ((p + k) % PAIRS) + c
        arrived(z, 1 - y, 0)
        arrived(z, 1 - y, 1)
        project(z, 1 - y)
        return 0

    lax.fori_loop(0, Z // 2, own_rows, 0)
    lax.fori_loop(1, PAIRS, other_rows, 0)
    arrived(2 * p + c, 1 - y, 0)
    arrived(2 * p + c, 1 - y, 1)
    own[...] = jnp.dot(
        abuf[p, :, 0].reshape(2 * rows, cols), wbuf[0], preferred_element_type=F32
    ) + jnp.dot(abuf[p, :, 1].reshape(2 * rows, cols), wbuf[1], preferred_element_type=F32)

    def add_in(k, _):
        src = (p + k) % PAIRS
        for yy in range(2):
            rc(
                sbuf.at[src, yy],
                rbuf.at[src, yy],
                s_p.at[src, yy],
                r_p.at[src, yy],
                me,
                2 * src + c,
            ).wait_recv()
            at = slice(yy * rows, (yy + 1) * rows)
            total = own[at] + rbuf[src, yy].astype(F32)
            if PAIRS == 2:
                out_ref[at] = total.astype(BF16)
            else:
                own[at] = total
        return 0

    if PAIRS == 2:
        add_in(1, 0)
    else:
        lax.fori_loop(1, PAIRS, add_in, 0)
        out_ref[...] = own[...].astype(BF16)

    t_own.wait_send()

    @pl.when(has_next)
    def _():
        t_next[0].wait_send()
        t_next[1].wait_send()

    w_remote.wait_send()

    def drain(z, _):
        doc = 2 * z + y
        send_y(own_block, doc).wait_send()
        send_sib(own_block, doc).wait_send()
        send_sib(own_block, 2 * z + 1 - y).wait_send()


        @pl.when(z % 2 == c)
        def _():
            for half in range(2):
                pl.when(z != zi)(lambda: fwd(z, half).wait_send())

            @pl.when(z // 2 != p)
            def _():
                for yy in range(2):
                    part_copy(z, yy).wait_send()

        return 0

    lax.fori_loop(0, Z, drain, 0)
    for k in range(1, Z):
        at_distance(k, lambda z: a_z(z).wait_send())
    a_y.wait_send()
    pl.when(t != c)(lambda: a_sib.wait_send())


def body(target_q, target_kv, doc_kv, doc_lengths, segment_ids, out_weight, ndoc, nhead):
    rows, cols = target_q.shape
    hd = target_kv.shape[1]
    slots = doc_kv.shape[1]
    wide = out_weight.shape[1]
    Z, pairs = ndoc // 2, nhead // 2
    vmem = pl.BlockSpec(memory_space=pltpu.VMEM)
    dma = pltpu.SemaphoreType.DMA
    flops = 4 * rows * cols * (ndoc * slots + 2 * rows) + 2 * ndoc * rows * cols * wide
    return pl.pallas_call(
        lambda *refs: kernel(ndoc, nhead, *refs),
        out_shape=jax.ShapeDtypeStruct((2 * rows, wide), BF16),
        in_specs=[pl.BlockSpec(memory_space=pltpu.HBM)] * 6,
        out_specs=vmem,
        scratch_shapes=[
            pltpu.SMEM((ndoc,), jnp.int32),
            pltpu.VMEM((ndoc, rows), jnp.int32),
            dma((4 + cols // hd,)),
            pltpu.VMEM((2, ndoc, slots, hd), BF16),
            pltpu.VMEM((2, 2 * rows, hd), BF16),
            pltpu.VMEM((2, cols, wide), BF16),
            pltpu.VMEM((cols // hd * rows, hd), BF16),
            pltpu.VMEM((1, cols // hd * rows), F32),
            pltpu.VMEM((1, cols // hd * rows), F32),
            pltpu.VMEM((hd, cols // hd * rows), F32),
            pltpu.VMEM((rows, cols), BF16),
            pltpu.VMEM((Z // 2, 2, 2, rows, cols), BF16),
            pltpu.VMEM((2 * rows, wide), F32),
            pltpu.VMEM((pairs, 2, rows, wide), BF16),
            pltpu.VMEM((pairs, 2, rows, wide), BF16),
            dma((Z,)),
            dma((ndoc,)),
            dma((ndoc,)),
            dma((ndoc,)),
            dma((ndoc,)),
            dma((3,)),
            dma((3,)),
            dma,
            dma,
            dma,
            dma((2,)),
            dma((Z,)),
            dma((Z // 2, 2)),
            dma((Z // 2, 2, 2)),
            dma((pairs, 2)),
            dma((pairs, 2)),
        ],
        compiler_params=pltpu.CompilerParams(
            collective_id=0, has_side_effects=True, vmem_limit_bytes=(64 << 20) - (1 << 16)
        ),
        cost_estimate=pl.CostEstimate(flops=flops, bytes_accessed=4 << 20, transcendentals=0),
    )(
        target_q,
        target_kv,
        doc_kv,
        doc_lengths,
        segment_ids.reshape(ndoc, rows),
        out_weight,
    )


def solution(mesh):
    ndoc, nhead = mesh.shape["doc"], mesh.shape["head"]
    placed = (
        P("doc", "head"),
        P("doc", "head"),
        P("doc", None, "head"),
        P(),
        P(),
        P("head", "doc"),
    )
    return jax.shard_map(
        lambda *args: body(*args, ndoc, nhead),
        mesh=mesh,
        in_specs=placed,
        out_specs=P("head", "doc"),
        check_vma=False,
    )
```

time: 57.2 us -> 49.9 us (0.87)
  the two profiles are of different devices: /device:TPU:3 before, /device:TPU:21 now
where the time goes in v2:
time: 49.9 us; the launch traced here: 49.4 us
  Pallas kernels  47.5 us (95%)
  local copies, waits for them, and re-layouts  1.87 us (4%)
    pallas_call x1, Pallas kernels, body(): pl.pallas_call(lambda *refs: kernel(ndoc, nhead, *refs), out_shape=jax.Sh...  47.5 us
    unnamed x1, local copies, waits for them, and re-layouts  1.87 us

profile of v2, /device:TPU:21, one launch (start us, length us, event | category | flops | bytes accessed | tf_op | source)
XLA Modules:
  0.0 49.4 jit_solution(6591977273205839110)
XLA Ops:
  0.0 47.5 %shard_map.64 = bf16[256,1024]{1,0:T(8,128)(2,1)} custom-call(bf16[128,512]{1,0:T(8,128)(2,1)} %refs_0_.1, bf16[128,128]{1,0:T(8,128)(2,1)} %refs_1_.1, bf16[1,384,128]{2,1,0:T(8,128)(2,1)} %refs_2_.1, s32[8]{0:T(128)} %refs_3_.1, s32[8,128]{1,0:T(8,128)} %bitcast.1, bf16[512,1024]{1,0:T(8,128)(2,1)} %refs_5_.1), custom_call_target="tpu_custom_call" | custom-call | flops 1946157056 | bytes 4194304 | tf_op jit(solution)/shard_map/pallas_call | solution.py:414
  47.5 1.9 %copy.8 = bf16[256,1024]{1,0:T(8,128)(2,1)} copy(bf16[256,1024]{1,0:T(8,128)(2,1)} %shard_map.64) | data formatting | bytes 1048576

commit v3 on v2

--- a/solution.py
+++ b/solution.py
@@ -1,3 +1,4 @@
+import itertools
 import math
 
 import jax
@@ -8,6 +9,7 @@
 from jax.sharding import PartitionSpec as P
 
 MASKED = -1e30
+PIECES = 2
 F32 = jnp.float32
 BF16 = jnp.bfloat16
 
@@ -65,6 +67,7 @@
     rows, cols = q_in.shape
     hd = tkv_in.shape[1]
     heads = cols // hd
+    piece = rows // PIECES
     Z = ndoc // 2
     PAIRS = nhead // 2
     me = lax.axis_index("doc")
@@ -268,19 +271,33 @@
         at = slice(j * rows, (j + 1) * rows)
         att[:, at] = (acc_s[:, at] / l_s[:, at]).T.astype(BF16)
 
-    def unit(z, yy, half):
-        return abuf.at[z // 2, yy, half]
-
-    a_sib = rc(att, unit(zi, y, c), s_a.at[0], r_a.at[zi // 2, y, c], me, sib)
-
-    def a_z(z):
-        return rc(att, unit(zi, y, c), s_az.at[z], r_a.at[zi // 2, y, c], 2 * z + y, owner)
-
-    a_y = rc(att, unit(zi, y, c), s_a.at[1], r_a.at[zi // 2, y, c], ynb, owner)
-    a_y.start()
-    for k in range(Z - 1, 0, -1):
-        at_distance(k, lambda z: a_z(z).start())
-    pl.when(t != c)(lambda: a_sib.start())
+    def unit(z, yy, half, r):
+        return abuf.at[z // 2, yy, half, pl.ds(r * piece, piece)]
+
+    def a_copy(r, sem, doc, head):
+        return rc(
+            att.at[pl.ds(r * piece, piece)],
+            unit(zi, y, c, r),
+            sem,
+            r_a.at[zi // 2, y, c, r],
+            doc,
+            head,
+        )
+
+    def a_sib(r):
+        return a_copy(r, s_a.at[0, r], me, sib)
+
+    def a_y(r):
+        return a_copy(r, s_a.at[1, r], ynb, owner)
+
+    def a_z(z, r):
+        return a_copy(r, s_az.at[z, r], 2 * z + y, owner)
+
+    for r in range(PIECES):
+        a_y(r).start()
+        for k in range(Z - 1, 0, -1):
+            at_distance(k, lambda z: a_z(z, r).start())
+        pl.when(t != c)(lambda: a_sib(r).start())
 
     @pl.when(t == c)
     def _():
@@ -289,72 +306,75 @@
     w_local.wait()
     w_remote.wait_recv()
 
-    def fwd(z, half):
-        block = unit(z, y, half)
-        return rc(block, block, s_ay.at[z // 2, half], r_a.at[z // 2, y, half], ynb, hi)
-
-    def arrived(z, yy, half):
-        rc(
-            unit(z, yy, half), unit(z, yy, half), s_a.at[0], r_a.at[z // 2, yy, half], ynb, hi
-        ).wait_recv()
-
-    def part_copy(z, yy):
-        return rc(sbuf.at[z // 2, yy], rbuf.at[p, yy], s_p.at[z // 2, yy], r_p.at[p, yy], me, z)
-
-    def project(z, yy):
-        part = jnp.dot(abuf[z // 2, yy, 0], wbuf[0], preferred_element_type=F32)
-        part = part + jnp.dot(abuf[z // 2, yy, 1], wbuf[1], preferred_element_type=F32)
-        sbuf[z // 2, yy] = part.astype(BF16)
-        part_copy(z, yy).start()
-
-    def place(k):
-        return 2 * ordered(zi // 2, Z // 2, k) + c
+    def fwd(z, half, r):
+        block = unit(z, y, half, r)
+        return rc(block, block, s_ay.at[z // 2, half, r], r_a.at[z // 2, y, half, r], ynb, hi)
+
+    def arrived(z, yy, half, r):
+        block = unit(z, yy, half, r)
+        rc(block, block, s_a.at[0, r], r_a.at[z // 2, yy, half, r], ynb, hi).wait_recv()
+
+    def part_copy(src, slot, yy, r, z):
+        at = pl.ds(r * piece, piece)
+        return rc(
+            sbuf.at[src, yy, at],
+            rbuf.at[slot, yy, at],
+            s_p.at[src, yy, r],
+            r_p.at[slot, yy, r],
+            me,
+            z,
+        )
+
+    def project(z, yy, r):
+        at = slice(r * piece, (r + 1) * piece)
+        part = jnp.dot(abuf[z // 2, yy, 0, at], wbuf[0], preferred_element_type=F32)
+        part = part + jnp.dot(abuf[z // 2, yy, 1, at], wbuf[1], preferred_element_type=F32)
+        sbuf[z // 2, yy, at] = part.astype(BF16)
+        part_copy(z // 2, p, yy, r, z).start()
 
     def own_rows(k, _):
         z = 2 * ((p + 1 + k) % PAIRS) + c
 
-        @pl.when(z == zi)
-        def _():
-            arrived(z, y, 1 - c)
-
-        for half in range(2):
-
-            @pl.when(z != zi)
+        for r in range(PIECES):
+
+            @pl.when(z == zi)
             def _():
-                arrived(z, y, half)
-                fwd(z, half).start()
-
-        pl.when(z // 2 != p)(lambda: project(z, y))
+                arrived(z, y, 1 - c, r)
+
+            for half in range(2):
+
+                @pl.when(z != zi)
+                def _():
+                    arrived(z, y, half, r)
+                    fwd(z, half, r).start()
+
+            pl.when(z // 2 != p)(lambda: project(z, y, r))
         return 0
 
     def other_rows(k, _):
         z = 2 * ((p + k) % PAIRS) + c
-        arrived(z, 1 - y, 0)
-        arrived(z, 1 - y, 1)
-        project(z, 1 - y)
+        for r in range(PIECES):
+            arrived(z, 1 - y, 0, r)
+            arrived(z, 1 - y, 1, r)
+            project(z, 1 - y, r)
         return 0
 
     lax.fori_loop(0, Z // 2, own_rows, 0)
     lax.fori_loop(1, PAIRS, other_rows, 0)
-    arrived(2 * p + c, 1 - y, 0)
-    arrived(2 * p + c, 1 - y, 1)
+    for r in range(PIECES):
+        arrived(2 * p + c, 1 - y, 0, r)
+        arrived(2 * p + c, 1 - y, 1, r)
     own[...] = jnp.dot(
         abuf[p, :, 0].reshape(2 * rows, cols), wbuf[0], preferred_element_type=F32
     ) + jnp.dot(abuf[p, :, 1].reshape(2 * rows, cols), wbuf[1], preferred_element_type=F32)
 
     def add_in(k, _):
         src = (p + k) % PAIRS
-        for yy in range(2):
-            rc(
-                sbuf.at[src, yy],
-                rbuf.at[src, yy],
-                s_p.at[src, yy],
-                r_p.at[src, yy],
-                me,
-                2 * src + c,
-            ).wait_recv()
-            at = slice(yy * rows, (yy + 1) * rows)
-            total = own[at] + rbuf[src, yy].astype(F32)
+        for yy, r in itertools.product(range(2), range(PIECES)):
+            part_copy(src, src, yy, r, 2 * src + c).wait_recv()
+            low = yy * rows + r * piece
+            at = slice(low, low + piece)
+            total = own[at] + rbuf[src, yy, r * piece : (r + 1) * piece].astype(F32)
             if PAIRS == 2:
                 out_ref[at] = total.astype(BF16)
             else:
@@ -385,21 +405,22 @@
 
         @pl.when(z % 2 == c)
         def _():
-            for half in range(2):
-                pl.when(z != zi)(lambda: fwd(z, half).wait_send())
+            for half, r in itertools.product(range(2), range(PIECES)):
+                pl.when(z != zi)(lambda: fwd(z, half, r).wait_send())
 
             @pl.when(z // 2 != p)
             def _():
-                for yy in range(2):
-                    part_copy(z, yy).wait_send()
+                for yy, r in itertools.product(range(2), range(PIECES)):
+                    part_copy(z // 2, p, yy, r, z).wait_send()
 
         return 0
 
     lax.fori_loop(0, Z, drain, 0)
-    for k in range(1, Z):
-        at_distance(k, lambda z: a_z(z).wait_send())
-    a_y.wait_send()
-    pl.when(t != c)(lambda: a_sib.wait_send())
+    for r in range(PIECES):
+        for k in range(1, Z):
+            at_distance(k, lambda z: a_z(z, r).wait_send())
+        a_y(r).wait_send()
+        pl.when(t != c)(lambda: a_sib(r).wait_send())
 
 
 def body(target_q, target_kv, doc_kv, doc_lengths, segment_ids, out_weight, ndoc, nhead):
@@ -442,12 +463,12 @@
             dma,
             dma,
             dma,
-            dma((2,)),
-            dma((Z,)),
-            dma((Z // 2, 2)),
-            dma((Z // 2, 2, 2)),
-            dma((pairs, 2)),
-            dma((pairs, 2)),
+            dma((2, PIECES)),
+            dma((Z, PIECES)),
+            dma((Z // 2, 2, PIECES)),
+            dma((Z // 2, 2, 2, PIECES)),
+            dma((pairs, 2, PIECES)),
+            dma((pairs, 2, PIECES)),
         ],
         compiler_params=pltpu.CompilerParams(
             collective_id=0, has_side_effects=True, vmem_limit_bytes=(64 << 20) - (1 << 16)

time: 49.9 us -> 48.5 us (0.972)
  Pallas kernels: 47.5 us -> 46.4 us
    pallas_call x1, Pallas kernels: 47.5 us -> 46.4 us  [body(): pl.pallas_call(lambda *refs: kernel(ndoc, nhead, *refs), out_shape=jax.Sh...]
where the time goes in v3:
time: 48.5 us; the launch traced here: 48.3 us
  Pallas kernels  46.4 us (96%)
  local copies, waits for them, and re-layouts  1.87 us (4%)
    pallas_call x1, Pallas kernels, body(): pl.pallas_call(lambda *refs: kernel(ndoc, nhead, *refs), out_shape=jax.Sh...  46.4 us
    unnamed x1, local copies, waits for them, and re-layouts  1.87 us

profile of v3, /device:TPU:21, one launch (start us, length us, event | category | flops | bytes accessed | tf_op | source)
XLA Modules:
  0.0 48.3 jit_solution(382835961766094685)
XLA Ops:
  0.0 46.4 %shard_map.64 = bf16[256,1024]{1,0:T(8,128)(2,1)} custom-call(bf16[128,512]{1,0:T(8,128)(2,1)} %refs_0_.1, bf16[128,128]{1,0:T(8,128)(2,1)} %refs_1_.1, bf16[1,384,128]{2,1,0:T(8,128)(2,1)} %refs_2_.1, s32[8]{0:T(128)} %refs_3_.1, s32[8,128]{1,0:T(8,128)} %bitcast.1, bf16[512,1024]{1,0:T(8,128)(2,1)} %refs_5_.1), custom_call_target="tpu_custom_call" | custom-call | flops 1946157056 | bytes 4194304 | tf_op jit(solution)/shard_map/pallas_call | solution.py:435
  46.4 1.9 %copy.8 = bf16[256,1024]{1,0:T(8,128)(2,1)} copy(bf16[256,1024]{1,0:T(8,128)(2,1)} %shard_map.64) | data formatting | bytes 1048576
